TPU v7x, 512 devices: a whole 4x8x8 slice. The times are simulated.
512 devices in a mesh: ga: 32 (over y_lo, z), band: 16 (over x, y_hi, core).
Axes of the slice: x: 4, y: 8 (y_hi: 2, y_lo: 4; y = y_hi * 4 + y_lo), z: 8, core: 2. Of those that a mesh axis runs over, the one named last changes fastest.
Arguments:
- becsum_part: float32 [16, 2048, 171], P('band'), may hold values from -0.03314563 to 0.03314563
- qrad: bfloat16 [2, 9, 128, 171], replicated, may hold values from -0.45703125 to 0.45703125
- positions: float32 [3, 2048], replicated, may hold values from 0 to 1
- species: int32 [2048], replicated, may hold values from 0 to 1
- miller: int32 [2, 512], P(None, 'ga'), may hold values from -192 to 191
Outputs:
- planes: float32 [2, 32, 16, 384], P(None, None, 'band', 'ga')
All inputs are finite; a program needn't handle non-finite values.
Results may differ from a plain program's by a relative error of at most 0.0046.
Values sent between devices are 32-bit elements; how exact they have to be, the bound alone decides.
A program may use at most 64 MiB of HBM per device.

v0:
```python
import math

import jax
import jax.numpy as jnp
from jax import lax
from jax.sharding import PartitionSpec as P

COL_DEV = 1
NZ = 384
NQ = 128


TWO_PI = 2.0 * math.pi


def species_columns(becsum, kinds, count):
    blocks = [becsum * (kinds == s).astype(becsum.dtype)[:, None] for s in range(count)]
    return jnp.concatenate(blocks, axis=1)


def arrange(qrad):
    nsp, nlm, nq, nij = qrad.shape
    even = jnp.concatenate([qrad[:, 0:1], qrad[:, 4:9]], axis=1)
    odd = qrad[:, 1:4]
    q_even = jnp.transpose(even, (1, 2, 0, 3)).reshape(6 * nq, nsp * nij)
    q_odd = jnp.transpose(odd, (1, 2, 0, 3)).reshape(3 * nq, nsp * nij)
    return (q_even, q_odd)


def frac(value):
    return value - jnp.floor(value)


def column_density(miller_pair, tau, bec_cols, q_even, q_odd, nz, nq):
    kidx = lax.iota(jnp.int32, nz)
    m_z = jnp.where(kidx < nz // 2, kidx, kidx - nz).astype(jnp.float32)
    m_x = miller_pair[0].astype(jnp.float32)
    m_y = miller_pair[1].astype(jnp.float32)
    part_x = frac(m_x * tau[0])
    part_y = frac(m_y * tau[1])
    part_z = frac(m_z[:, None] * tau[2][None, :])
    theta = TWO_PI * (part_z + (part_x + part_y)[None, :])
    cos_part = jnp.cos(theta).astype(jnp.bfloat16)
    sin_part = jnp.sin(theta).astype(jnp.bfloat16)
    b_cos = jnp.dot(cos_part, bec_cols, preferred_element_type=jnp.float32)
    b_sin = jnp.dot(sin_part, bec_cols, preferred_element_type=jnp.float32)
    gnorm = jnp.sqrt(m_x * m_x + m_y * m_y + m_z * m_z)
    inverse = 1.0 / jnp.maximum(gnorm, 1.0)
    unit_x = m_x * inverse
    unit_y = m_y * inverse
    unit_z = m_z * inverse
    root3 = math.sqrt(3.0)
    ones = jnp.ones_like(unit_z)
    even = jnp.stack(
        [
            ones,
            -root3 * unit_x * unit_y,
            -root3 * unit_y * unit_z,
            -root3 * unit_z * unit_x,
            -0.5 * root3 * (unit_x * unit_x - unit_y * unit_y) * ones,
            -0.5 * (3.0 * unit_z * unit_z - 1.0),
        ],
        axis=1,
    )
    odd = jnp.stack([-unit_x * ones, -unit_y * ones, -unit_z], axis=1)
    tpos = gnorm * ((nq - 1) / (math.sqrt(3.0) * nz / 2.0))
    table = lax.iota(jnp.int32, nq).astype(jnp.float32)
    hat = jnp.maximum(0.0, 1.0 - jnp.abs(tpos[:, None] - table[None, :]))
    w_even = (even[:, :, None] * hat[:, None, :]).reshape(nz, 6 * nq).astype(jnp.bfloat16)
    w_odd = (odd[:, :, None] * hat[:, None, :]).reshape(nz, 3 * nq).astype(jnp.bfloat16)
    q_re = jnp.dot(w_even, q_even, preferred_element_type=jnp.float32)
    q_im = jnp.dot(w_odd, q_odd, preferred_element_type=jnp.float32)
    real_part = jnp.sum(q_re * b_cos + q_im * b_sin, axis=1)
    imag_part = jnp.sum(q_im * b_cos - q_re * b_sin, axis=1)
    return jnp.stack([real_part, imag_part])


def transform(dens):
    kidx = lax.iota(jnp.int32, NZ)
    product = kidx[:, None] * kidx[None, :] % NZ
    angle = TWO_PI * product.astype(jnp.float32) / NZ
    cos_table = jnp.cos(angle)
    sin_table = jnp.sin(angle)
    scale = 1.0 / math.sqrt(NZ)
    highest = lax.Precision.HIGHEST
    real_part = jnp.dot(dens[0], cos_table, precision=highest) - jnp.dot(
        dens[1], sin_table, precision=highest
    )
    imag_part = jnp.dot(dens[0], sin_table, precision=highest) + jnp.dot(
        dens[1], cos_table, precision=highest
    )
    return jnp.stack([real_part * scale, imag_part * scale])


def planes_of(columns):
    moved = lax.all_to_all(columns, "ga", split_axis=2, concat_axis=1, tiled=True)
    return moved.reshape(2, lax.axis_size("ga"), columns.shape[1], moved.shape[2])


def becsum_whole(becsum_part):
    return lax.psum(becsum_part[0], "band")


def species_rounded(total, kinds, count):
    return species_columns(total, kinds, count).astype(jnp.bfloat16)


def densities(miller_cols, tau, bec_cols, q_even, q_odd):

    def one_column(miller_pair):
        return column_density(miller_pair, tau, bec_cols, q_even, q_odd, NZ, NQ)

    dens = lax.map(one_column, jnp.transpose(miller_cols))
    return jnp.transpose(dens, (1, 0, 2))


def per_device(becsum_part, qrad, positions, species, miller):
    count = qrad.shape[0]
    q_even, q_odd = arrange(qrad)
    member = lax.axis_index("band")
    bec_cols = species_rounded(becsum_whole(becsum_part), species, count)
    mine = lax.dynamic_slice_in_dim(miller, member * COL_DEV, COL_DEV, 1)
    dens = densities(mine, positions, bec_cols, q_even, q_odd)
    return planes_of(transform(dens))


def solution(mesh):
    placed = (P("band", None, None), P(), P(), P(), P(None, "ga"))
    return jax.shard_map(
        per_device,
        mesh=mesh,
        in_specs=placed,
        out_specs=P(None, None, "band", "ga"),
        check_vma=False,
    )
```

profile of v0, /device:TPU:1, one launch (start us, length us, event | category | flops | bytes accessed | tf_op | source)
XLA Modules:
  0.0 276.1 jit_solution(1802551888375060223)
XLA Ops:
  6.5 0.0 copy-start
  6.5 0.0 all-reduce.2.cloned.1.call-start
  6.5 3.0 %copy.22 = f32[1,2048,171]{1,2,0:T(8,128)} copy(f32[1,2048,171]{1,0,2:T(1,128)} %param.5) | data formatting | bytes 2801664
  9.5 0.0 copy-start.1
  9.5 0.0 all-reduce.2.cloned.1.call-update
  9.6 0.0 copy-done
  9.6 0.1 constant_dynamic-slice_fusion
  9.7 0.6 fusion.61
  11.7 0.0 copy-done.1
  11.7 0.2 slice_bitcast_fusion
  11.9 0.0 slice-start
  11.9 0.0 slice-start.1
  11.9 0.1 copy.14
  12.1 0.1 pad.10
  12.3 0.7 slice-done
  12.9 0.0 slice-done.1
  13.0 0.7 maximum_bitcast_fusion
  13.6 0.1 copy.13
  13.8 0.0 copy-start.3
  13.8 0.1 pad.9
  13.9 0.1 copy.19
  14.0 0.0 copy-start.2
  14.0 0.1 subtract_maximum_fusion
  14.2 0.3 copy-done.3
  14.5 0.1 multiply_convert_fusion.2
  14.6 0.4 fusion.62
  15.0 0.0 copy-done.2
  15.0 190.9 %all-reduce.2.cloned.1.call-done = f32[2048,171]{0,1:T(8,128)} async-done(((f32[2048,171]{0,1:T(8,128)}), f32[2048,171]{0,1:T(8,128)}) %all-reduce.2.cloned.1.call-update) | async-done | bytes 1400848 | tf_op jit(solution)/shard_map/psum | solution.py:101
  205.9 1.6 multiply_convert_fusion.1
  207.5 11.5 %fusion.3 = f32[384,342]{0,1:T(8,128)S(1)} fusion(f32[2048]{0:T(1024)S(1)} %bitcast.46, f32[2048]{0:T(1024)S(1)} %bitcast.44, f32[384]{0:T(512)S(1)} %fusion.36, bf16[2048,171]{0,1:T(8,128)(2,1)S(1)} %get-tuple-element.20, bf16[2048,171]{0,1:T(8,128)(2,1)S(1)} %get-tuple-element.19), kind=kOutput, calls=%fused_computation.6 | convolution fusion | flops 545439744 | bytes 1944064 | tf_op jit(solution)/shard_map/while/body/eval_jaxpr/dot_general | solution.py:46
  219.0 21.2 %fusion.2 = f32[384,342]{0,1:T(8,128)S(1)} fusion(f32[2048]{0:T(1024)S(1)} %bitcast.47, f32[2048]{0:T(1024)S(1)} %bitcast.45, f32[384]{0:T(512)S(1)} %fusion.36, bf16[2048,171]{0,1:T(8,128)(2,1)S(1)} %get-tuple-element.20, bf16[2048,171]{0,1:T(8,128)(2,1)S(1)} %get-tuple-element.19), kind=kOutput, calls=%fused_computation.5 | convolution fusion | flops 545439744 | bytes 1944064 | tf_op jit(solution)/shard_map/while/body/eval_jaxpr/dot_general | solution.py:45
  240.2 0.5 subtract_reduce_fusion
  240.8 2.7 convolution_reduce_fusion.1
  243.5 2.7 convolution_reduce_fusion.3
  246.1 2.7 convolution_reduce_fusion
  248.8 2.7 convolution_reduce_fusion.2
  251.6 0.1 copy.15
  251.7 16.5 %all_to_all.4 = f32[2,1,384]{0,1,2:T(1,128)S(1)} all-to-all(f32[2,1,384]{0,1,2:T(1,128)S(1)} %copy.15), channel_id=1, replica_groups=mesh['ga'=32,'band'=16] {'ga'}, dimensions={2} | all-to-all | bytes 6144 | tf_op jit(solution)/shard_map/all_to_all | solution.py:96
  268.2 0.1 copy.16
  268.2 0.1 reshape.216
  268.4 0.7 copy.17
  (21 shorter events, 0.3 us)
Async XLA Ops:
  6.5 3.1 %copy-start = (s32[2,16]{1,0:T(2,128)S(1)}, s32[2,16]{1,0:T(2,128)}, u32[]{:S(2)}) copy-start(s32[2,16]{1,0:T(2,128)} %param.9) | copy-start | bytes 388
  6.5 199.4 %all-reduce.2.cloned.1.call-start = ((), (), s32[]{:S(2)}) async-start(), calls=%async_computation.1 | async-start | bytes 2883584 | tf_op jit(solution)/shard_map/psum | solution.py:101
  9.5 2.2 copy-start.1
  11.9 1.0 slice-start
  11.9 1.0 slice-start.1
  13.8 0.7 copy-start.3
  14.0 1.0 copy-start.2
Sparse Core Ops, SparseCore 0:
  10.3 195.5 all-reduce.1
where the time goes:
time: 282 us; the launch traced here: 276 us
  waiting for transfers between devices  191 us (68%)
  matrix products  44.3 us (16%)
  blocking collectives  16.5 us (6%)
  between operations  15.2 us (5%)
  local copies, waits for them, and re-layouts  6.55 us (2%)
    psum x1, waiting for transfers between devices, becsum_whole(): return lax.psum(becsum_part[0], 'band')  191 us
    dot_general x1, matrix products, column_density(): b_cos = jnp.dot(cos_part, bec_cols, preferred_element_type=jnp.float32)  21.2 us
    all_to_all x1, blocking collectives, planes_of(): lax.all_to_all(columns, 'ga', split_axis=2, concat_axis=1, tiled=True)  16.5 us
    dot_general x1, matrix products, column_density(): b_sin = jnp.dot(sin_part, bec_cols, preferred_element_type=jnp.float32)  11.5 us
  transfers between devices with their start and end apart: 1, of which 1 were waited for; matrix products, arithmetic and copies ran while one was open for 1% of the time, Pallas kernels for 0%

commit v1 on v0

v1 whole, which is shorter than its diff:
```python
import math

import jax
import jax.numpy as jnp
import numpy as np
from jax import lax
from jax.experimental import pallas as pl
from jax.experimental.pallas import tpu as pltpu
from jax.sharding import PartitionSpec as P

MESH = pl.DeviceIdType.MESH
F32 = jnp.float32
BF16 = jnp.bfloat16

NZ = 384
NQ = 128
NLM = 9
NSP = 2
NIJ = 171
N_GA = 32
N_BAND = 16
ATOMS = 64
HALF_IJ = 96
OWNERS = HALF_IJ // 8
M = 256
PLANES = NZ // N_GA
HALF_Z = PLANES // 2
ROOT3 = math.sqrt(3.0)

COS_TERMS = (
    0.9999999890590227, -19.73920449945391, 64.93911745989556, -85.45013953088247,
    60.16763095094928, -25.967599248494622, 6.528658161366808,
)
SIN_TERMS = (
    6.283185302511503, -41.341700405317496, 81.60513138579344, -76.70301535379849,
    42.025926985567956, -14.89984666736486, 3.238137509743233,
)


def transform_table():
    table = np.zeros((2, N_GA, 8, 2, M))
    m = np.arange(NZ // 2 + 1)
    factor = np.where(m == 0, 1.0, 2.0)
    factor[NZ // 2] = 1.0
    for half in range(2):
        for i in range(HALF_Z):
            z = PLANES * np.arange(N_GA) + HALF_Z * half + i
            angle = 2.0 * np.pi * ((z[:, None] * m[None, :]) % NZ) / NZ
            table[half, :, i, 0, : m.size] = factor * np.cos(angle) / math.sqrt(NZ)
            table[half, :, i, 1, : m.size] = factor * np.sin(angle) / math.sqrt(NZ)
    table = table.reshape(2, N_GA * 8, 2 * M).astype(np.float32)
    high = table.astype(BF16)
    return np.stack([high, (table - high.astype(np.float32)).astype(BF16)])


def frac(value):
    return value - jnp.floor(value)


def cos_sin(turns):
    r = turns - jnp.floor(turns + 0.5)
    r2 = r * r
    c = jnp.full_like(r, COS_TERMS[-1])
    s = jnp.full_like(r, SIN_TERMS[-1])
    for k in range(len(COS_TERMS) - 2, -1, -1):
        c = c * r2 + COS_TERMS[k]
        s = s * r2 + SIN_TERMS[k]
    return c, s * r


def kernel(
    bec_ref, q_ref, pos_ref, spec_ref, mil_ref, dft_ref, out_ref,
    part, got, whole, mil_out, mil_in, waves, coef, hats, trig, lhs, table_z, terms, dens, planes, landed, q_vmem, dft_vmem,
    rs_send, rs_recv, ag_send, ag_recv, mil_send, mil_recv, out_send, out_recv, load,
):
    g = lax.axis_index("ga")
    b = lax.axis_index("band")

    def band_peer(d):
        return lax.rem(b + d, N_BAND)

    def ga_peer(d):
        return lax.rem(g + d, N_GA)

    q_copy = pltpu.make_async_copy(q_ref, q_vmem, load.at[0])
    q_copy.start()
    dft_copy = pltpu.make_async_copy(dft_ref, dft_vmem, load.at[1])
    dft_copy.start()

    barrier = pltpu.get_barrier_semaphore()

    @pl.loop(1, N_BAND)
    def _(d):
        pl.semaphore_signal(barrier, inc=1, device_id=(g, band_peer(d)), device_id_type=MESH)

    @pl.loop(1, N_GA)
    def _(d):
        pl.semaphore_signal(barrier, inc=1, device_id=(ga_peer(d), b), device_id_type=MESH)

    part[...] = bec_ref[...]
    lane16 = lax.broadcasted_iota(jnp.int32, (2, 16), 1)
    own = jnp.sum(jnp.where(lane16 == b, mil_ref[...].astype(F32), 0.0), axis=1, keepdims=True)
    tile = jnp.concatenate([jnp.broadcast_to(own, (2, 128)), jnp.zeros((6, 128), F32)], axis=0)
    mil_out[...] = tile
    mil_in[g] = tile

    pl.semaphore_wait(barrier, N_BAND - 1 + N_GA - 1)

    @pl.loop(0, OWNERS)
    def _(p):
        @pl.when(p != b)
        def _():
            pltpu.make_async_remote_copy(
                src_ref=part.at[p], dst_ref=got.at[b], send_sem=rs_send, recv_sem=rs_recv,
                device_id=(g, p), device_id_type=MESH,
            ).start()

    @pl.loop(1, N_GA)
    def _(d):
        pltpu.make_async_remote_copy(
            src_ref=mil_out, dst_ref=mil_in.at[g], send_sem=mil_send, recv_sem=mil_recv,
            device_id=(ga_peer(d), b), device_id_type=MESH,
        ).start()

    at = pl.multiple_of(lax.div(g, 2) * 128, 128)
    tau = pos_ref[:, pl.ds(at, 128)]
    kind = spec_ref[:, pl.ds(at, 128)].astype(F32)
    atoms = jnp.concatenate([tau, kind, jnp.zeros((4, 128), F32)], axis=0)
    atoms = jnp.where(lax.rem(g, 2) == 0, atoms, pltpu.roll(atoms, 64, axis=1))
    by_atom = jnp.transpose(jnp.concatenate([atoms, jnp.zeros((120, 128), F32)], axis=0))[:ATOMS]
    m_at = lax.broadcasted_iota(jnp.int32, (1, M), 1)
    m_z = m_at.astype(F32)
    cos_z, sin_z = cos_sin(frac(by_atom[:, 2:3] * m_z))
    table_z[0] = cos_z
    table_z[1] = sin_z

    @pl.when(b < OWNERS)
    def _():
        got[b] = part[b]
        pltpu.make_async_copy(got.at[pl.ds(0, N_BAND - 1)], got.at[pl.ds(0, N_BAND - 1)], rs_recv).wait()
        whole[b] = jnp.sum(got[...], axis=0)

        @pl.loop(1, N_BAND)
        def _(d):
            pltpu.make_async_remote_copy(
                src_ref=whole.at[b], dst_ref=whole.at[b], send_sem=ag_send, recv_sem=ag_recv,
                device_id=(g, band_peer(d)), device_id_type=MESH,
            ).start()

    pltpu.make_async_copy(mil_in.at[pl.ds(0, N_GA - 1)], mil_in.at[pl.ds(0, N_GA - 1)], mil_recv).wait()
    m_x = mil_in[:, 0, :]
    m_y = mil_in[:, 1, :]
    rho2 = m_x * m_x + m_y * m_y
    rho2_wide = jnp.concatenate([rho2, rho2], axis=1)
    gnorm = jnp.sqrt(rho2_wide + m_z * m_z)
    inverse = 1.0 / jnp.maximum(gnorm, 1.0)
    inverse2 = inverse * inverse
    waves[0] = gnorm * ((NQ - 1) / (ROOT3 * NZ / 2.0))
    waves[1] = jnp.where(rho2_wide > 0.0, inverse2, jnp.where(m_at == 0, 1.0, 0.0))
    waves[2] = inverse
    waves[3] = m_z * inverse2
    waves[4] = m_z * inverse
    coef[0] = -ROOT3 * m_x * m_y
    coef[1] = (-0.5 * ROOT3) * (m_x * m_x - m_y * m_y)
    coef[2] = 1.5 * jnp.maximum(rho2, 1.0)
    coef[3] = -ROOT3 * m_x
    coef[4] = -ROOT3 * m_y
    coef[5] = -m_x
    coef[6] = -m_y
    phase_cos, phase_sin = cos_sin(frac(m_x * atoms[0:1]) + frac(m_y * atoms[1:2]))
    rest = jnp.zeros((128 - N_GA, 128), F32)
    phase_cos = jnp.transpose(jnp.concatenate([phase_cos, rest], axis=0))[:ATOMS]
    phase_sin = jnp.transpose(jnp.concatenate([phase_sin, rest], axis=0))[:ATOMS]
    point = lax.broadcasted_iota(jnp.int32, (NQ, M), 0).astype(F32)

    @pl.loop(0, N_GA)
    def _(c):
        t = waves[0, pl.ds(c, 1), :]
        hats[c] = jnp.maximum(0.0, 1.0 - jnp.abs(t - point)).astype(BF16)
        turn = lax.rem(128 - c, 128)
        c_f = pltpu.roll(phase_cos, turn, axis=1)[:, 0:1]
        s_f = pltpu.roll(phase_sin, turn, axis=1)[:, 0:1]
        cc = table_z[0] * c_f
        ss = table_z[1] * s_f
        sc = table_z[1] * c_f
        cs = table_z[0] * s_f
        for k, part_of in enumerate((cc - ss, cs + sc, cc + ss, cs - sc)):
            trig[c, k] = part_of.astype(BF16).astype(F32)

    @pl.when(b < OWNERS)
    def _():
        pltpu.make_async_copy(whole.at[pl.ds(0, OWNERS - 1)], whole.at[pl.ds(0, OWNERS - 1)], ag_recv).wait()

    @pl.when(b >= OWNERS)
    def _():
        pltpu.make_async_copy(whole, whole, ag_recv).wait()

    q_copy.wait()
    becsum = whole[...].reshape(HALF_IJ, 128)
    becsum = jnp.concatenate([becsum, jnp.zeros((128 - HALF_IJ, 128), F32)], axis=0)
    becsum = jnp.transpose(becsum)[:, :HALF_IJ].astype(BF16)
    kinds = by_atom[:, 3:4]
    total = jnp.zeros((ATOMS, NLM * NQ), F32)
    for s in range(NSP):
        mask = jnp.where(kinds == float(s), 1.0, 0.0).astype(BF16)
        for h in range(2):
            rows = becsum[h * ATOMS : (h + 1) * ATOMS] * mask
            total = total + jnp.dot(rows, q_vmem[s, h], preferred_element_type=F32)
    for e in range(NLM):
        terms[e] = total[:, e * NQ : (e + 1) * NQ]
    lhs[pl.ds(0, ATOMS)] = (terms[0] - terms[8]).astype(BF16)
    lhs[pl.ds(4 * ATOMS, ATOMS)] = (-terms[3]).astype(BF16)
    last = m_at == NZ // 2

    @pl.loop(0, N_GA)
    def _(c):
        def scalar(k):
            return coef[k, pl.ds(c, 1), :]

        def wave(k):
            return waves[k, pl.ds(c, 1), :]

        lhs[pl.ds(ATOMS, ATOMS)] = (scalar(0) * terms[4] + scalar(1) * terms[7] + scalar(2) * terms[8]).astype(BF16)
        lhs[pl.ds(2 * ATOMS, ATOMS)] = (scalar(4) * terms[5] + scalar(3) * terms[6]).astype(BF16)
        lhs[pl.ds(3 * ATOMS, ATOMS)] = (scalar(5) * terms[1] + scalar(6) * terms[2]).astype(BF16)
        at_g = jnp.dot(lhs[...], hats[c], preferred_element_type=F32)
        re_even = at_g[:ATOMS] + wave(1) * at_g[ATOMS : 2 * ATOMS]
        re_odd = wave(3) * at_g[2 * ATOMS : 3 * ATOMS]
        im_even = wave(2) * at_g[3 * ATOMS : 4 * ATOMS]
        im_odd = wave(4) * at_g[4 * ATOMS :]

        def summed(x):
            return jnp.sum(x, axis=0, keepdims=True)

        re, im = re_even + re_odd, im_even + im_odd
        re_up = summed(re * trig[c, 0] + im * trig[c, 1])
        im_up = summed(im * trig[c, 0] - re * trig[c, 1])
        re, im = re_even - re_odd, im_even - im_odd
        re_down = summed(re * trig[c, 2] + im * trig[c, 3])
        im_down = summed(im * trig[c, 2] - re * trig[c, 3])
        re_up = jnp.where(last, re_down, re_up)
        im_up = jnp.where(last, im_down, im_up)
        dens[pl.ds(c, 1), pl.ds(0, M)] = 0.5 * (re_up + re_down)
        dens[pl.ds(c, 1), pl.ds(M, M)] = -0.5 * (im_up - im_down)
        dens[pl.ds(N_GA + c, 1), pl.ds(0, M)] = 0.5 * (im_up + im_down)
        dens[pl.ds(N_GA + c, 1), pl.ds(M, M)] = 0.5 * (re_up - re_down)

    dft_copy.wait()
    high = dens[...].astype(BF16)
    low = (dens[...] - high.astype(F32)).astype(BF16)

    def against(rows, columns):
        return lax.dot_general(rows, columns, (((1,), (1,)), ((), ())), preferred_element_type=F32)

    halves = [
        against(dft_vmem[0, h], high) + (against(dft_vmem[0, h], low) + against(dft_vmem[1, h], high))
        for h in range(2)
    ]
    planes[...] = jnp.concatenate(halves, axis=1).reshape(N_GA, 8, 128)

    @pl.loop(1, N_GA)
    def _(d):
        peer = ga_peer(d)
        pltpu.make_async_remote_copy(
            src_ref=planes.at[peer], dst_ref=landed.at[g], send_sem=out_send, recv_sem=out_recv,
            device_id=(peer, b), device_id_type=MESH,
        ).start()

    landed[g] = planes[g]
    pltpu.make_async_copy(landed.at[pl.ds(0, N_GA - 1)], landed.at[pl.ds(0, N_GA - 1)], out_recv).wait()
    mine = jnp.sum(landed[...], axis=0)
    for r in range(2):
        for h in range(2):
            first = h * 64 + r * 32
            out_ref[pl.ds(r * PLANES + h * HALF_Z, HALF_Z), :] = mine[:HALF_Z, first : first + N_GA]

    pltpu.make_async_copy(mil_in.at[pl.ds(0, N_GA - 1)], mil_in.at[pl.ds(0, N_GA - 1)], mil_send).wait()
    pltpu.make_async_copy(landed.at[pl.ds(0, N_GA - 1)], landed.at[pl.ds(0, N_GA - 1)], out_send).wait()

    @pl.when(b < OWNERS)
    def _():
        pltpu.make_async_copy(part.at[pl.ds(0, OWNERS - 1)], part.at[pl.ds(0, OWNERS - 1)], rs_send).wait()
        pltpu.make_async_copy(got.at[pl.ds(0, N_BAND - 1)], got.at[pl.ds(0, N_BAND - 1)], ag_send).wait()

    @pl.when(b >= OWNERS)
    def _():
        pltpu.make_async_copy(part, part, rs_send).wait()


def arranged(qrad):
    q = jnp.transpose(qrad, (0, 3, 1, 2)).reshape(NSP, NIJ, NLM * NQ)
    q = jnp.pad(q, ((0, 0), (0, 2 * HALF_IJ - NIJ), (0, 0)))
    return q.reshape(NSP, 2, HALF_IJ, NLM * NQ)


def per_device(becsum_part, qrad, positions, species, miller):
    g = lax.axis_index("ga")
    pairs = jnp.transpose(becsum_part[0])
    mine = lax.dynamic_slice_in_dim(pairs, g * ATOMS, ATOMS, 1)
    mine = jnp.pad(mine, ((0, 2 * HALF_IJ - NIJ), (0, 0)))
    mine = jnp.concatenate([mine[:HALF_IJ], mine[HALF_IJ:]], axis=1).reshape(OWNERS, 8, 128)
    vmem = pl.BlockSpec(memory_space=pltpu.VMEM)
    hbm = pl.BlockSpec(memory_space=pl.ANY)
    planes = pl.pallas_call(
        kernel,
        out_shape=jax.ShapeDtypeStruct((2 * PLANES, N_GA), F32),
        in_specs=[vmem, hbm, vmem, vmem, vmem, hbm],
        out_specs=vmem,
        scratch_shapes=[
            pltpu.VMEM((OWNERS, 8, 128), F32),
            pltpu.VMEM((N_BAND, 8, 128), F32),
            pltpu.VMEM((OWNERS, 8, 128), F32),
            pltpu.VMEM((8, 128), F32),
            pltpu.VMEM((N_GA, 8, 128), F32),
            pltpu.VMEM((5, N_GA, M), F32),
            pltpu.VMEM((7, N_GA, 128), F32),
            pltpu.VMEM((N_GA, NQ, M), BF16),
            pltpu.VMEM((N_GA, 4, ATOMS, M), F32),
            pltpu.VMEM((5 * ATOMS, NQ), BF16),
            pltpu.VMEM((2, ATOMS, M), F32),
            pltpu.VMEM((NLM, ATOMS, NQ), F32),
            pltpu.VMEM((2 * N_GA, 2 * M), F32),
            pltpu.VMEM((N_GA, 8, 128), F32),
            pltpu.VMEM((N_GA, 8, 128), F32),
            pltpu.VMEM((NSP, 2, HALF_IJ, NLM * NQ), BF16),
            pltpu.VMEM((2, 2, N_GA * 8, 2 * M), BF16),
        ]
        + [pltpu.SemaphoreType.DMA] * 8
        + [pltpu.SemaphoreType.DMA((2,))],
        compiler_params=pltpu.CompilerParams(
            collective_id=0, has_side_effects=True, vmem_limit_bytes=40 * 2**20
        ),
    )(mine, arranged(qrad), positions, species.reshape(1, -1), miller, jnp.asarray(transform_table()))
    return jnp.transpose(planes.reshape(2, PLANES, N_GA), (0, 2, 1)).reshape(2, N_GA, 1, PLANES)


def solution(mesh):
    placed = (P("band", None, None), P(), P(), P(), P(None, "ga"))
    return jax.shard_map(
        per_device,
        mesh=mesh,
        in_specs=placed,
        out_specs=P(None, None, "band", "ga"),
        check_vma=False,
    )
```

time: 282 us -> 51.6 us (0.18); the launches traced: 276 us -> 51.4 us
  waiting for transfers between devices: 191 us -> 0 us
  Pallas kernels: 0 us -> 44.8 us
  matrix products: 44.3 us -> 0 us
  blocking collectives: 16.5 us -> 0 us
  between operations: 15.2 us -> 0.06 us
    psum x1 -> x0, waiting for transfers between devices: 191 us -> none  [becsum_whole(): return lax.psum(becsum_part[0], 'band')]
    pallas_call x0 -> x1, Pallas kernels: none -> 44.8 us  [per_device(): pl.pallas_call(kernel, out_shape=jax.ShapeDtypeStruct((2 * PLANES, N_GA),...]
    dot_general x8 -> x0, matrix products: 44.3 us -> none  [the longest x1 21.2 us: column_density(): b_cos = jnp.dot(cos_part, bec_cols, preferred_element_type=jnp.float32)]
    all_to_all x1 -> x0, blocking collectives: 16.5 us -> none  [planes_of(): lax.all_to_all(columns, 'ga', split_axis=2, concat_axis=1, tiled=True)]
  transfers between devices with their start and end apart: 1 -> 0, of which waited for: 1 -> 0; matrix products, arithmetic and copies ran while one was open for 1% -> 0% of each run, Pallas kernels for 0% -> 0%
where the time goes in v1:
time: 51.6 us; the launch traced here: 51.4 us
  Pallas kernels  44.8 us (87%)
  local copies, waits for them, and re-layouts  6.55 us (13%)
    pallas_call x1, Pallas kernels, per_device(): pl.pallas_call(kernel, out_shape=jax.ShapeDtypeStruct((2 * PLANES, N_GA),...  44.8 us
    unnamed x11, local copies, waits for them, and re-layouts  1.6 us
    transpose x1, local copies, waits for them, and re-layouts, arranged(): q = jnp.transpose(qrad, (0, 3, 1, 2)).reshape(NSP, NIJ, NLM * NQ)  1.37 us
    pad x1, local copies, waits for them, and re-layouts, arranged(): q = jnp.pad(q, ((0, 0), (0, 2 * HALF_IJ - NIJ), (0, 0)))  1.3 us
    reshape x1, local copies, waits for them, and re-layouts, arranged(): q = jnp.transpose(qrad, (0, 3, 1, 2)).reshape(NSP, NIJ, NLM * NQ)  1.27 us

profile of v1, /device:TPU:1, one launch (start us, length us, event | category | flops | bytes accessed | tf_op | source)
XLA Modules:
  0.0 51.4 jit_solution(6213187143124959577)
XLA Ops:
  0.0 0.0 copy-start
  0.0 1.3 %copy-done = f32[1,2048,171]{1,0,2:T(1,128)S(1)} copy-done((f32[1,2048,171]{1,0,2:T(1,128)S(1)}, f32[1,2048,171]{1,0,2:T(1,128)}, u32[]{:S(2)}) %copy-start) | copy-done | bytes 1400856
  1.3 0.2 constant_dynamic-slice_fusion
  1.6 0.1 copy.14
  1.7 0.1 fusion
  1.8 0.1 copy.8
  1.9 1.4 %copy.9 = bf16[2,171,9,128]{3,2,1,0:T(8,128)(2,1)S(1)} copy(bf16[2,171,9,128]{3,0,1,2:T(2,128)(2,1)} %bitcast.13) | data formatting | bytes 1575936 | tf_op jit(solution)/shard_map/transpose | solution.py:291
  3.2 1.3 %reshape.23 = bf16[2,171,1152]{2,1,0:T(8,128)(2,1)} reshape(bf16[2,171,9,128]{3,2,1,0:T(8,128)(2,1)S(1)} %copy.9) | data formatting | bytes 1575936 | tf_op jit(solution)/shard_map/reshape | solution.py:291
  4.5 0.0 copy-start.1
  4.5 0.0 copy-start.2
  4.5 0.0 copy-start.3
  4.5 0.0 copy-start.4
  4.5 1.3 %pad.9 = bf16[2,192,1152]{2,1,0:T(8,128)(2,1)S(1)} pad(bf16[2,171,1152]{2,1,0:T(8,128)(2,1)} %reshape.23, bf16[]{:T(256)} %constant.18.clone.1), padding=0_0x0_21x0_0 | pad | bytes 1672706 | tf_op jit(solution)/shard_map/jit(_pad)/pad | solution.py:292
  5.8 0.2 copy-done.1
  6.0 0.0 copy-done.2
  6.0 0.0 copy-done.3
  6.0 0.0 copy-done.4
  6.0 44.8 %shard_map.64 = f32[24,32]{1,0:T(8,128)S(1)} custom-call(f32[12,8,128]{2,1,0:T(8,128)S(1)} %bitcast.11, bf16[2,2,96,1152]{3,2,1,0:T(8,128)(2,1)S(1)} %bitcast.10, f32[3,2048]{1,0:T(4,128)S(1)} %copy-done.2, s32[1,2048]{1,0:T(1,128)S(1)} %bitcast.12, s32[2,16]{1,0:T(2,128)S(1)} %copy-done.4, bf16[2,2,256,512]{3,2,1,0:T(8,128)(2,1)S(1)} %copy-done.1), custom_call_target="tpu_custom_call" | custom-call | tf_op jit(solution)/shard_map/pallas_call | solution.py:304
  50.8 0.6 %copy.11 = f32[2,32,1,12]{1,2,3,0:T(1,128)} copy(f32[2,32,1,12]{1,3,0,2:T(8,128)S(1)} %bitcast.15) | data formatting | bytes 6144 | tf_op jit(solution)/shard_map/reshape | solution.py:334
  (2 shorter events, 0.0 us)
Async XLA Ops:
  0.0 1.3 %copy-start = (f32[1,2048,171]{1,0,2:T(1,128)S(1)}, f32[1,2048,171]{1,0,2:T(1,128)}, u32[]{:S(2)}) copy-start(f32[1,2048,171]{1,0,2:T(1,128)} %param.6) | copy-start | bytes 4202500
  4.5 1.5 %copy-start.1 = (bf16[2,2,256,512]{3,2,1,0:T(8,128)(2,1)S(1)}, bf16[2,2,256,512]{3,2,1,0:T(8,128)(2,1)}, u32[]{:S(2)}) copy-start(bf16[2,2,256,512]{3,2,1,0:T(8,128)(2,1)} %constant.19.clone.dft_ref) | copy-start | bytes 3145732
  4.5 1.5 %copy-start.2 = (f32[3,2048]{1,0:T(4,128)S(1)}, f32[3,2048]{1,0:T(4,128)}, u32[]{:S(2)}) copy-start(f32[3,2048]{1,0:T(4,128)} %pos_ref.1) | copy-start | bytes 73732
  4.5 1.5 %copy-start.3 = (s32[2048]{0:T(1024)S(1)}, s32[2048]{0:T(1024)}, u32[]{:S(2)}) copy-start(s32[2048]{0:T(1024)} %param.9) | copy-start | bytes 24580
  4.5 1.5 %copy-start.4 = (s32[2,16]{1,0:T(2,128)S(1)}, s32[2,16]{1,0:T(2,128)}, u32[]{:S(2)}) copy-start(s32[2,16]{1,0:T(2,128)} %mil_ref.1) | copy-start | bytes 388
